TPU v7x, 32 devices: a whole 2x2x4 slice. The times are simulated.
32 devices in a mesh: tile: 8 (over y, x, core), mode: 4 (over z).
Axes of the slice: x: 2, y: 2, z: 4, core: 2. Of those that a mesh axis runs over, the one named last changes fastest.
Arguments:
- object_field: float32 [2, 4096, 384], P(None, 'tile'), may hold values from -4 to 4
- probe: float32 [4, 2, 256, 256], P('mode'), may hold values from -3 to 3
- intensities: bfloat16 [32, 256, 256], P('tile'), may hold values from 0.049804688 to 8
- scan_rows: int32 [32], P('tile'), may hold values from 0 to 511
- scan_cols: int32 [32], P('tile'), may hold values from 0 to 127
Outputs:
- updated_object: float32 [2, 4096, 384], P(None, 'tile')
- position_step: float32 [32, 2], P('tile')
All inputs are finite; a program needn't handle non-finite values.
Results may differ from a plain program's by a relative error of at most 0.0003.
Values sent between devices are 32-bit elements; how exact they have to be, the bound alone decides.
A program may use at most 64 MiB of HBM per device.

v0:
```python
import functools
import math

import jax
import jax.numpy as jnp
import numpy as np
from jax import lax
from jax.experimental import pallas as pl
from jax.experimental.pallas import tpu as pltpu
from jax.sharding import PartitionSpec as P

damping = 0.5
F32 = jnp.float32
BF16 = jnp.bfloat16


def from_behind(value, axis, steps):
    count = lax.axis_size(axis)
    first, last = (max(0, -steps), min(count, count - steps))
    return lax.ppermute(value, axis, [(source, source + steps) for source in range(first, last)])


def tables(side):
    half = side // 2
    k = np.arange(half)
    stack = []
    for odd in (0, 1):
        turn = (k[:, None] * (2 * k[None, :] + odd)) % side
        w = np.exp(-2j * math.pi * turn / side) / math.sqrt(side)
        real = np.block([[w.real, w.imag], [-w.imag, w.real]]).astype(np.float32)
        for table in (real, real.T):
            high = table.astype(jnp.bfloat16)
            low = (table - high.astype(np.float32)).astype(jnp.bfloat16)
            stack += [high, low]
    order = np.concatenate([np.arange(0, side, 2), np.arange(1, side, 2)])
    move = np.zeros((side, side), np.float32)
    move[np.arange(side), order] = 1.0
    stack += [move.astype(jnp.bfloat16), move.T.astype(jnp.bfloat16)]
    return np.stack(stack)


def split(x):
    high = x.astype(BF16)
    return high, (x - high.astype(F32)).astype(BF16)


def times(x, high, low):
    a, b = split(x)
    return jnp.dot(
        jnp.concatenate([a, b, a], axis=1),
        jnp.concatenate([high, high, low], axis=0),
        preferred_element_type=F32,
    )


def under(high, low, x):
    a, b = split(x)
    return jnp.dot(
        jnp.concatenate([high, high, low], axis=1),
        jnp.concatenate([a, b, a], axis=0),
        preferred_element_type=F32,
    )


def compute_kernel(
    rows_ref, cols_ref, prev_rows_ref, prev_cols_ref, ext, probe, measured, table,
    frame, light, stats, win, far, inten, pad, lightpad, lightbuf,
):
    positions = rows_ref.shape[0]
    modes, _, side, _ = probe.shape
    half = side // 2
    columns = ext.shape[2]
    tile_rows = light.shape[0]
    span = win.shape[1]

    def tab(odd, flip):
        i = 4 * odd + 2 * flip
        return table[i], table[i + 1]

    frame[...] = jnp.zeros_like(frame)
    lightbuf[...] = jnp.zeros_like(lightbuf)
    pad[...] = jnp.zeros_like(pad)
    lightpad[...] = jnp.zeros_like(lightpad)
    illumination = jnp.zeros((side, side), F32)
    for m in range(modes):
        illumination += probe[m, 0] * probe[m, 0] + probe[m, 1] * probe[m, 1]
    lightpad[:side, :side] = illumination

    def add_light(r, c, base):
        low = lax.rem(r, 8)
        at = pl.multiple_of(base + r - low, 8)
        x = pltpu.roll(pltpu.roll(lightpad[...], c, 1), low, 0)
        lightbuf[pl.ds(at, span), :] += x

    @pl.loop(0, positions)
    def _(p):
        add_light(rows_ref[p], cols_ref[p], tile_rows)
        add_light(prev_rows_ref[p], prev_cols_ref[p], 0)

    light[...] = lightbuf[tile_rows : 2 * tile_rows, :]

    @pl.loop(0, positions)
    def _(p):
        r = rows_ref[p]
        c = cols_ref[p]
        low = lax.rem(r, 8)
        base = pl.multiple_of(r - low, 8)
        for ch in range(2):
            x = ext[ch, pl.ds(base, span + 8), :]
            x = pltpu.roll(x, lax.rem(columns - c, columns), 1)
            x = pltpu.roll(x, lax.rem(span + 8 - low, span + 8), 0)
            win[ch] = x[:span]
        inten[...] = jnp.zeros_like(inten)

        @pl.loop(0, modes)
        def _(m):
            pr, pi = probe[m, 0], probe[m, 1]
            wr, wi = win[0, :side, :side], win[1, :side, :side]
            xr = pr * wr - pi * wi
            xi = pr * wi + pi * wr
            even = under(*tab(0, 1), jnp.concatenate([xr[:half] + xr[half:], xi[:half] + xi[half:]], 0))
            odd = under(*tab(1, 1), jnp.concatenate([xr[:half] - xr[half:], xi[:half] - xi[half:]], 0))
            sums, diffs = [], []
            for part in (even, odd):
                a, b = part[:, :half] + part[:, half:], part[:, :half] - part[:, half:]
                sums.append(jnp.concatenate([a[:half], a[half:]], 1))
                diffs.append(jnp.concatenate([b[:half], b[half:]], 1))
            fe = times(jnp.concatenate(sums, 0), *tab(0, 0))
            fo = times(jnp.concatenate(diffs, 0), *tab(1, 0))
            far[m, 0] = fe
            far[m, 1] = fo
            inten[:, :half] += fe[:, :half] * fe[:, :half] + fe[:, half:] * fe[:, half:]
            inten[:, half:] += fo[:, :half] * fo[:, :half] + fo[:, half:] * fo[:, half:]

        moved = jnp.dot(table[8], measured[p], preferred_element_type=F32).astype(BF16)
        moved = jnp.dot(moved, table[9], preferred_element_type=F32)
        inten[...] = jnp.sqrt(moved) / jnp.sqrt(jnp.maximum(inten[...], 0.25)) - 1.0
        pad[:, :side, :side] = jnp.zeros((2, side, side), F32)

        @pl.loop(0, modes)
        def _(m):
            se, so = inten[:, :half], inten[:, half:]
            u = times(far[m, 0] * jnp.concatenate([se, se], 1), *tab(0, 1))
            v = times(far[m, 1] * jnp.concatenate([so, so], 1), *tab(1, 1))
            a, b = u + v, u - v
            yr = jnp.concatenate([a[:, :half], b[:, :half]], 1)
            yi = jnp.concatenate([a[:, half:], b[:, half:]], 1)
            u = under(*tab(0, 0), jnp.concatenate([yr[:half], yi[:half]], 0))
            v = under(*tab(1, 0), jnp.concatenate([yr[half:], yi[half:]], 0))
            a, b = u + v, u - v
            cr = jnp.concatenate([a[:half], b[:half]], 0)
            ci = jnp.concatenate([a[half:], b[half:]], 0)
            pr, pi = probe[m, 0], probe[m, 1]
            pad[0, :side, :side] += pr * cr + pi * ci
            pad[1, :side, :side] += pr * ci - pi * cr

        gr, gi = pad[0, :side, :side], pad[1, :side, :side]
        wr, wi = win[0, :side, :side], win[1, :side, :side]
        shine = lightpad[:side, :side]
        for d in range(2):
            if d == 0:
                dr, di = win[0, 1 : side + 1, :side] - wr, win[1, 1 : side + 1, :side] - wi
            else:
                dr = pltpu.roll(win[0, :side, :], columns - 1, 1)[:, :side] - wr
                di = pltpu.roll(win[1, :side, :], columns - 1, 1)[:, :side] - wi
            stats[p, d : d + 1, :] = jnp.sum(dr * gr + di * gi, axis=0, keepdims=True)
            stats[p, d + 2 : d + 3, :] = jnp.sum((dr * dr + di * di) * shine, axis=0, keepdims=True)
        for ch in range(2):
            x = pltpu.roll(pltpu.roll(pad[ch], c, 1), low, 0)
            frame[ch, pl.ds(base, span), :] += x


def on_device(object_field, probe, intensities, scan_rows, scan_cols):
    tile_rows, columns = object_field.shape[1:]
    side = probe.shape[-1]
    positions = scan_rows.shape[0]
    modes = lax.axis_size("mode")
    span = side + 8
    following = from_behind(object_field[:, :side, :], "tile", -1)
    extended = jnp.concatenate(
        [object_field, following, jnp.zeros((2, 16, columns), F32)], axis=1
    )
    probes = lax.all_gather(probe, "mode", axis=0, tiled=True)
    prev_rows, prev_cols = from_behind((scan_rows, scan_cols), "tile", 1)
    smem = pl.BlockSpec(memory_space=pltpu.SMEM)
    vmem = pl.BlockSpec(memory_space=pltpu.VMEM)
    frame, light, stats = pl.pallas_call(
        compute_kernel,
        out_shape=(
            jax.ShapeDtypeStruct((2, tile_rows + side, columns), F32),
            jax.ShapeDtypeStruct((tile_rows, columns), F32),
            jax.ShapeDtypeStruct((positions, 4, side), F32),
        ),
        in_specs=[smem] * 4 + [vmem] * 4,
        out_specs=(vmem, vmem, vmem),
        scratch_shapes=[
            pltpu.VMEM((2, span, columns), F32),
            pltpu.VMEM((modes, 2, side, side), F32),
            pltpu.VMEM((side, side), F32),
            pltpu.VMEM((2, span, columns), F32),
            pltpu.VMEM((span, columns), F32),
            pltpu.VMEM((2 * tile_rows + side, columns), F32),
        ],
        compiler_params=pltpu.CompilerParams(vmem_limit_bytes=48 * 1024 * 1024),
    )(scan_rows, scan_cols, prev_rows, prev_cols, extended, probes, intensities, jnp.asarray(tables(side)))
    pixels = side * side
    terms = jnp.sum(stats, axis=2) / pixels / modes
    position_step = terms[:, :2] / (terms[:, 2:] + 1e-06)
    carried = from_behind(frame[:, tile_rows:], "tile", 1)
    own_grad = frame[:, :tile_rows].at[:, :side].add(carried)
    updated_object = object_field + own_grad / (light + damping)[None]
    return (updated_object, position_step)


def solution(mesh):
    in_specs = (
        P(None, "tile", None),
        P("mode", None, None, None),
        P("tile", None, None),
        P("tile"),
        P("tile"),
    )
    out_specs = (P(None, "tile", None), P("tile", None))
    return jax.shard_map(
        on_device, mesh=mesh, in_specs=in_specs, out_specs=out_specs, check_vma=False
    )
```

profile of v0, /device:TPU:4, one launch (start us, length us, event | category | flops | bytes accessed | tf_op | source)
XLA Modules:
  0.0 121.4 jit_solution(466855159596900040)
XLA Ops:
  7.2 0.0 copy-start.3
  7.2 0.0 copy-start.4
  7.2 0.0 all-gather.2.cloned.1.call-start
  7.2 0.7 all-gather.2.cloned.1.call-update
  7.9 0.0 copy-start.5
  7.9 1.3 %slice.40 = f32[2,256,384]{2,1,0:T(8,128)S(1)} slice(f32[2,512,384]{2,1,0:T(8,128)} %param.8), slice={[0:2], [0:256], [0:384]} | slice | bytes 1572864 | tf_op jit(solution)/shard_map/slice | solution.py:179
  9.2 2.8 %collective-permute-start.2 = (f32[2,256,384]{2,1,0:T(8,128)S(1)}, f32[2,256,384]{2,1,0:T(8,128)S(1)}, u32[]{:S(2)}, u32[]{:S(2)}) collective-permute-start(f32[2,256,384]{2,1,0:T(8,128)S(1)} %slice.40), channel_id=1, source_target_pairs={{4,0},{8,4},{12,8},{16,12},{20,16},{24,20},{28,24},{5,1},{9,5},{13... | collective-permute-start | bytes 2359304 | tf_op jit(solution)/shard_map/ppermute | solution.py:20
  12.0 0.0 copy-done.3
  12.0 1.9 %collective-permute-start = (s32[4]{0:T(128)S(1)}, s32[4]{0:T(128)S(1)}, u32[]{:S(2)}, u32[]{:S(2)}) collective-permute-start(s32[4]{0:T(128)S(1)} %copy-done.3), channel_id=1, source_target_pairs={{0,4},{4,8},{8,12},{12,16},{16,20},{20,24},{24,28},{1,5},{5,9},{9,... | collective-permute-start | bytes 56 | tf_op jit(solution)/shard_map/ppermute | solution.py:20
  14.0 0.0 copy-done.4
  14.0 2.6 %collective-permute-start.1 = (s32[4]{0:T(128)S(1)}, s32[4]{0:T(128)S(1)}, u32[]{:S(2)}, u32[]{:S(2)}) collective-permute-start(s32[4]{0:T(128)S(1)} %copy-done.4), channel_id=1, source_target_pairs={{0,4},{4,8},{8,12},{12,16},{16,20},{20,24},{24,28},{1,5},{5,9},{9,... | collective-permute-start | bytes 56 | tf_op jit(solution)/shard_map/ppermute | solution.py:20
  16.7 0.0 copy-start.1
  16.7 0.0 copy-start.2
  16.7 4.9 %collective-permute-done.2 = f32[2,256,384]{2,1,0:T(8,128)S(1)} collective-permute-done((f32[2,256,384]{2,1,0:T(8,128)S(1)}, f32[2,256,384]{2,1,0:T(8,128)S(1)}, u32[]{:S(2)}, u32[]{:S(2)}) %collective-permute-start.2) | collective-permute-done | bytes 786464 | tf_op jit(solution)/shard_map/ppermute | solution.py:20
  21.5 0.0 copy-done.5
  21.5 1.7 %maximum_maximum_fusion.ext = f32[2,784,384]{2,1,0:T(8,128)} fusion(f32[2,256,384]{2,1,0:T(8,128)S(1)} %collective-permute-done.2, f32[2,512,384]{2,1,0:T(8,128)S(1)} %copy-done.5, f32[784]{0:T(1024)S(1)} %pad.4.clone), kind=kLoop, calls=%fused_computation | loop fusion | flops 1204224 | bytes 4770880 | tf_op jit(solution)/shard_map/concatenate | solution.py:180
  23.2 0.0 collective-permute-done.prev_rows_ref
  23.2 0.0 collective-permute-done.1.prev_cols_ref
  23.2 33.6 %all-gather.2.cloned.1.call-done.probe = f32[4,2,256,256]{3,2,1,0:T(8,128)} async-done(((f32[1,2,256,256]{3,2,1,0:T(8,128)}), f32[4,2,256,256]{3,2,1,0:T(8,128)}) %all-gather.2.cloned.1.call-update) | async-done | bytes 2097168 | tf_op jit(solution)/shard_map/all_gather | solution.py:183
  56.8 1.6 %copy-done = f32[4,2,256,256]{3,2,1,0:T(8,128)S(1)} copy-done((f32[4,2,256,256]{3,2,1,0:T(8,128)S(1)}, f32[4,2,256,256]{3,2,1,0:T(8,128)}, u32[]{:S(2)}) %copy-start) | copy-done | bytes 2097176
  58.4 38.2 %shard_map.77 = (f32[2,768,384]{2,1,0:T(8,128)}, f32[512,384]{1,0:T(8,128)S(1)}, f32[4,4,256]{2,1,0:T(4,128)S(1)}) custom-call(s32[4]{0:T(128)S(1)} %copy-done.3, s32[4]{0:T(128)S(1)} %copy-done.4, s32[4]{0:T(128)S(1)} %collective-permute-done.prev_rows_ref, s32[4]{0:T(128)S(1)} %collective-permute-done.1.prev_cols_ref, ...), custom_call_target="tpu_custom_call" | custom-call | tf_op jit(solution)/shard_map/pallas_call | solution.py:187
  96.6 1.2 slice.43
  97.8 1.9 %collective-permute-start.3 = (f32[2,256,384]{2,1,0:T(8,128)S(1)}, f32[2,256,384]{2,1,0:T(8,128)S(1)}, u32[]{:S(2)}, u32[]{:S(2)}) collective-permute-start(f32[2,256,384]{2,1,0:T(8,128)S(1)} %slice.43), channel_id=1, source_target_pairs={{0,4},{4,8},{8,12},{12,16},{16,20},{20,24},{24,28},{1,5},{5,9},{9,... | collective-permute-start | bytes 2359304 | tf_op jit(solution)/shard_map/ppermute | solution.py:20
  99.7 2.7 %slice.41 = f32[2,512,384]{2,1,0:T(8,128)} slice(f32[2,768,384]{2,1,0:T(8,128)} %get-tuple-element.17), slice={[0:2], [0:512], [0:384]} | slice | bytes 3145728 | tf_op jit(solution)/shard_map/slice | solution.py:210
  102.4 0.1 reduce_sum.9
  102.5 0.1 add_divide_fusion
  102.5 0.7 copy.8
  103.2 0.1 broadcast_add_fusion
  103.3 0.0 copy-start.6
  103.3 8.7 %collective-permute-done.3 = f32[2,256,384]{2,1,0:T(8,128)S(1)} collective-permute-done((f32[2,256,384]{2,1,0:T(8,128)S(1)}, f32[2,256,384]{2,1,0:T(8,128)S(1)}, u32[]{:S(2)}, u32[]{:S(2)}) %collective-permute-start.3) | collective-permute-done | bytes 786464 | tf_op jit(solution)/shard_map/ppermute | solution.py:20
  112.0 1.2 add_dynamic-update-slice_fusion
  113.2 1.3 %divide_add_fusion = f32[2,512,384]{2,1,0:T(8,128)} fusion(f32[2,512,384]{2,1,0:T(8,128)S(1)} %copy-done.6, f32[2,512,384]{2,1,0:T(8,128)S(1)} %add_dynamic-update-slice_fusion, f32[512,384]{1,0:T(8,128)S(1)} %broadcast_add_fusion), kind=kLoop, calls=%fused_computation.1 | loop fusion | flops 786432 | bytes 5505024 | tf_op jit(solution)/shard_map/add | solution.py:211
  (9 shorter events, 0.0 us)
Async XLA Ops:
  7.2 4.9 %copy-start.3 = (s32[4]{0:T(128)S(1)}, s32[4]{0:T(128)}, u32[]{:S(2)}) copy-start(s32[4]{0:T(128)} %rows_ref.1) | copy-start | bytes 52
  7.2 6.8 %copy-start.4 = (s32[4]{0:T(128)S(1)}, s32[4]{0:T(128)}, u32[]{:S(2)}) copy-start(s32[4]{0:T(128)} %cols_ref.1) | copy-start | bytes 52
  7.2 49.6 %all-gather.2.cloned.1.call-start = ((), (), s32[]{:S(2)}) async-start(), calls=%async_computation | async-start | bytes 2621440 | tf_op jit(solution)/shard_map/all_gather | solution.py:183
  7.9 13.6 %copy-start.5 = (f32[2,512,384]{2,1,0:T(8,128)S(1)}, f32[2,512,384]{2,1,0:T(8,128)}, u32[]{:S(2)}) copy-start(f32[2,512,384]{2,1,0:T(8,128)} %param.8) | copy-start | bytes 4718596
  9.2 12.3 %collective-permute-start.2 = (f32[2,256,384]{2,1,0:T(8,128)S(1)}, f32[2,256,384]{2,1,0:T(8,128)S(1)}, u32[]{:S(2)}, u32[]{:S(2)}) collective-permute-start(f32[2,256,384]{2,1,0:T(8,128)S(1)} %slice.40), channel_id=1, source_target_pairs={{4,0},{8,4},{12,8},{16,12},{20,16},{24,20},{28,24},{5,1},{9,5},{13... | collective-permute-start | bytes 2359304 | tf_op jit(solution)/shard_map/ppermute | solution.py:20
  12.0 11.2 %collective-permute-start = (s32[4]{0:T(128)S(1)}, s32[4]{0:T(128)S(1)}, u32[]{:S(2)}, u32[]{:S(2)}) collective-permute-start(s32[4]{0:T(128)S(1)} %copy-done.3), channel_id=1, source_target_pairs={{0,4},{4,8},{8,12},{12,16},{16,20},{20,24},{24,28},{1,5},{5,9},{9,... | collective-permute-start | bytes 56 | tf_op jit(solution)/shard_map/ppermute | solution.py:20
  14.0 9.2 %collective-permute-start.1 = (s32[4]{0:T(128)S(1)}, s32[4]{0:T(128)S(1)}, u32[]{:S(2)}, u32[]{:S(2)}) collective-permute-start(s32[4]{0:T(128)S(1)} %copy-done.4), channel_id=1, source_target_pairs={{0,4},{4,8},{8,12},{12,16},{16,20},{20,24},{24,28},{1,5},{5,9},{9,... | collective-permute-start | bytes 56 | tf_op jit(solution)/shard_map/ppermute | solution.py:20
  16.7 40.1 %copy-start.1 = (bf16[10,256,256]{2,1,0:T(8,128)(2,1)S(1)}, bf16[10,256,256]{2,1,0:T(8,128)(2,1)}, u32[]{:S(2)}) copy-start(bf16[10,256,256]{2,1,0:T(8,128)(2,1)} %constant.42.clone.table) | copy-start | bytes 3932164
  16.7 40.1 %copy-start.2 = (bf16[4,256,256]{2,1,0:T(8,128)(2,1)S(1)}, bf16[4,256,256]{2,1,0:T(8,128)(2,1)}, u32[]{:S(2)}) copy-start(bf16[4,256,256]{2,1,0:T(8,128)(2,1)} %measured.1) | copy-start | bytes 1572868
  56.8 1.6 %copy-start = (f32[4,2,256,256]{3,2,1,0:T(8,128)S(1)}, f32[4,2,256,256]{3,2,1,0:T(8,128)}, u32[]{:S(2)}) copy-start(f32[4,2,256,256]{3,2,1,0:T(8,128)} %all-gather.2.cloned.1.call-done.probe) | copy-start | bytes 6291460
  97.8 14.2 %collective-permute-start.3 = (f32[2,256,384]{2,1,0:T(8,128)S(1)}, f32[2,256,384]{2,1,0:T(8,128)S(1)}, u32[]{:S(2)}, u32[]{:S(2)}) collective-permute-start(f32[2,256,384]{2,1,0:T(8,128)S(1)} %slice.43), channel_id=1, source_target_pairs={{0,4},{4,8},{8,12},{12,16},{16,20},{20,24},{24,28},{1,5},{5,9},{9,... | collective-permute-start | bytes 2359304 | tf_op jit(solution)/shard_map/ppermute | solution.py:20
  103.2 8.8 %copy-start.7 = (f32[2,512,384]{2,1,0:T(8,128)S(1)}, f32[2,512,384]{2,1,0:T(8,128)}, u32[]{:S(2)}) copy-start(f32[2,512,384]{2,1,0:T(8,128)} %slice.41) | copy-start | bytes 4718596
  103.3 10.0 %copy-start.6 = (f32[2,512,384]{2,1,0:T(8,128)S(1)}, f32[2,512,384]{2,1,0:T(8,128)}, u32[]{:S(2)}) copy-start(f32[2,512,384]{2,1,0:T(8,128)} %param.8) | copy-start | bytes 4718596
Sparse Core Ops, SparseCore 0:
  9.6 47.1 all-gather.1
where the time goes:
time: 122 us; the launch traced here: 121 us
  waiting for transfers between devices  47.8 us (39%)
  Pallas kernels  38.2 us (31%)
  between operations  14.2 us (12%)
  starting transfers between devices  9.3 us (8%)
  local copies, waits for them, and re-layouts  7.44 us (6%)
  other arithmetic  4.44 us (4%)
    pallas_call x1, Pallas kernels, on_device(): pl.pallas_call(compute_kernel, out_shape=(jax.ShapeDtypeStruct((2, tile_r...  38.2 us
    all_gather x1, waiting for transfers between devices, on_device(): probes = lax.all_gather(probe, 'mode', axis=0, tiled=True)  33.6 us
    ppermute x4, waiting for transfers between devices, from_behind(): lax.ppermute(value, axis, [(source, source + steps) for source in range(f...  13.6 us
    ppermute x4, starting transfers between devices, from_behind(): lax.ppermute(value, axis, [(source, source + steps) for source in range(f...  9.26 us
    slice x1, local copies, waits for them, and re-layouts, on_device(): own_grad = frame[:, :tile_rows].at[:, :side].add(carried)  2.66 us
  transfers between devices with their start and end apart: 5, of which 3 were waited for; matrix products, arithmetic and copies ran while one was open for 5% of the time, Pallas kernels for 0%

commit v1 on v0

v1 whole, which is shorter than its diff:
```python
import math

import jax
import jax.numpy as jnp
import numpy as np
from jax import lax
from jax.experimental import pallas as pl
from jax.experimental.pallas import tpu as pltpu
from jax.sharding import PartitionSpec as P

damping = 0.5
F32 = jnp.float32
BF16 = jnp.bfloat16
MESH = pl.DeviceIdType.MESH


def tables(side):
    half = side // 2
    k = np.arange(half)
    stack = []
    for odd in (0, 1):
        turn = (k[:, None] * (2 * k[None, :] + odd)) % side
        w = np.exp(-2j * math.pi * turn / side) / math.sqrt(side)
        real = np.block([[w.real, w.imag], [-w.imag, w.real]]).astype(np.float32)
        for table in (real, real.T):
            high = table.astype(jnp.bfloat16)
            low = (table - high.astype(np.float32)).astype(jnp.bfloat16)
            stack += [high, low]
    order = np.concatenate([np.arange(0, side, 2), np.arange(1, side, 2)])
    move = np.zeros((side, side), np.float32)
    move[np.arange(side), order] = 1.0
    stack += [move.astype(jnp.bfloat16), move.T.astype(jnp.bfloat16)]
    return np.stack(stack)


def split(x):
    high = x.astype(BF16)
    return high, (x - high.astype(F32)).astype(BF16)


def times(x, high, low):
    a, b = split(x)
    return jnp.dot(
        jnp.concatenate([a, b, a], axis=1),
        jnp.concatenate([high, high, low], axis=0),
        preferred_element_type=F32,
    )


def under(high, low, x):
    a, b = split(x)
    return jnp.dot(
        jnp.concatenate([high, high, low], axis=1),
        jnp.concatenate([a, b, a], axis=0),
        preferred_element_type=F32,
    )


def to(t, z):
    return dict(device_id=(t, z), device_id_type=MESH)


def gather_kernel(
    own, probe, scan_rows, scan_cols, following, probes, prev_rows, prev_cols,
    z_send, z_recv, y_send, y_recv, c_send, c_recv, h_send, h_recv, own_sem,
):
    tile, mode = lax.axis_index("tile"), lax.axis_index("mode")
    tiles, modes = lax.axis_size("tile"), lax.axis_size("mode")
    side = probe.shape[-1]
    half = side // 2
    core = lax.rem(tile, 2)
    sibling = tile + 1 - 2 * core
    upper = lax.rem(tile // 4, 2)
    across = tile + 4 - 8 * upper
    part = pl.ds(pl.multiple_of(upper * half, half), half)
    after, before = lax.rem(tile + 1, tiles), lax.rem(tile + tiles - 1, tiles)

    barrier = pltpu.get_barrier_semaphore()
    greeted = [(after, mode), (before, mode), (across, mode)]
    greeted += [(tile, lax.rem(mode + k, modes)) for k in range(1, modes)]
    for t, z in greeted:
        pl.semaphore_signal(barrier, inc=1, **to(t, z))
    pl.semaphore_wait(barrier, len(greeted))

    halo = pltpu.make_async_remote_copy(
        src_ref=own.at[:, :side, :], dst_ref=following,
        send_sem=h_send.at[0], recv_sem=h_recv.at[0], **to(before, mode))
    send_rows = pltpu.make_async_remote_copy(
        src_ref=scan_rows, dst_ref=prev_rows,
        send_sem=h_send.at[1], recv_sem=h_recv.at[1], **to(after, mode))
    send_cols = pltpu.make_async_remote_copy(
        src_ref=scan_cols, dst_ref=prev_cols,
        send_sem=h_send.at[2], recv_sem=h_recv.at[2], **to(after, mode))

    def over_modes(k):
        return pltpu.make_async_remote_copy(
            src_ref=probe.at[0, core, part, :], dst_ref=probes.at[mode, core, part, :],
            send_sem=z_send.at[k - 1], recv_sem=z_recv.at[k - 1], **to(tile, lax.rem(mode + k, modes)))

    def source(k):
        return lax.rem(mode + modes - k, modes)

    def over_y(k):
        at = probes.at[source(k), core, part, :]
        return pltpu.make_async_remote_copy(
            src_ref=at, dst_ref=at, send_sem=y_send.at[k - 1], recv_sem=y_recv.at[k - 1], **to(across, mode))

    def over_core(k):
        at = probes.at[source(k), core]
        return pltpu.make_async_remote_copy(
            src_ref=at, dst_ref=at, send_sem=c_send.at[k - 1], recv_sem=c_recv.at[k - 1], **to(sibling, mode))

    order = [k for k in (1, 3, 2) if k < modes] + list(range(4, modes))
    for k in order:
        over_modes(k).start()
    pl.when(tile > 0)(halo.start)
    send_rows.start()
    send_cols.start()
    keep = pltpu.make_async_copy(probe.at[0], probes.at[mode], own_sem.at[0])
    keep.start()
    for k in order:
        over_modes(k).wait_recv()
        over_y(k).start()
    for k in order:
        over_y(k).wait_recv()
        over_core(k).start()
    for k in order:
        over_core(k).wait_recv()
    keep.wait()
    pl.when(tile < tiles - 1)(halo.wait_recv)
    pl.when(tile > 0)(halo.wait_send)
    send_rows.wait()
    send_cols.wait()
    for k in order:
        over_modes(k).wait_send()
        over_y(k).wait_send()
        over_core(k).wait_send()


def compute_kernel(
    rows_ref, cols_ref, prev_rows_ref, prev_cols_ref, own, following, probes, measured, table,
    frame, light, steps, ext, win, far, inten, pad, lightpad, lightbuf, nums, dens, load_sem,
):
    tile, tiles = lax.axis_index("tile"), lax.axis_size("tile")
    positions = rows_ref.shape[0]
    modes, _, side, _ = probes.shape
    half = side // 2
    tile_rows, columns = own.shape[1:]
    span = win.shape[2]

    def tab(odd, flip):
        i = 4 * odd + 2 * flip
        return table[i], table[i + 1]

    load_own = pltpu.make_async_copy(own, ext.at[:, :tile_rows, :], load_sem.at[0])
    load_next = pltpu.make_async_copy(
        following, ext.at[:, tile_rows : tile_rows + side, :], load_sem.at[1])
    load_own.start()
    pl.when(tile < tiles - 1)(load_next.start)
    ext[:, tile_rows + side :, :] = jnp.zeros((2, ext.shape[1] - tile_rows - side, columns), F32)

    @pl.when(tile == tiles - 1)
    def _():
        ext[:, tile_rows : tile_rows + side, :] = jnp.zeros((2, side, columns), F32)

    for ref in (frame, lightbuf, pad, lightpad, inten):
        ref[...] = jnp.zeros_like(ref)
    illumination = jnp.zeros((side, side), F32)
    for m in range(modes):
        illumination += probes[m, 0] * probes[m, 0] + probes[m, 1] * probes[m, 1]
    lightpad[:side, :side] = illumination

    def add_light(r, c, base):
        low = lax.rem(r, 8)
        at = pl.multiple_of(base + r - low, 8)
        x = pltpu.roll(pltpu.roll(lightpad[...], c, 1), low, 0)
        lightbuf[pl.ds(at, span), :] += x

    @pl.loop(0, positions)
    def _(p):
        add_light(rows_ref[p], cols_ref[p], tile_rows)
        first = tile == 0
        add_light(jnp.where(first, 0, prev_rows_ref[p]), jnp.where(first, 0, prev_cols_ref[p]), 0)

    load_own.wait()
    pl.when(tile < tiles - 1)(load_next.wait)

    @pl.loop(0, positions)
    def _(p):
        r, c = rows_ref[p], cols_ref[p]
        low = lax.rem(r, 8)
        base = pl.multiple_of(r - low, 8)
        for ch in range(2):
            x = ext[ch, pl.ds(base, span + 8), :]
            x = pltpu.roll(x, lax.rem(columns - c, columns), 1)
            win[p, ch] = pltpu.roll(x, lax.rem(span + 8 - low, span + 8), 0)[:span]

    light[...] = lightbuf[tile_rows : 2 * tile_rows, :]

    def forward(p, m):
        pr, pi = probes[m, 0], probes[m, 1]
        wr, wi = win[p, 0, :side, :side], win[p, 1, :side, :side]
        xr = pr * wr - pi * wi
        xi = pr * wi + pi * wr
        even = under(*tab(0, 1), jnp.concatenate([xr[:half] + xr[half:], xi[:half] + xi[half:]], 0))
        odd = under(*tab(1, 1), jnp.concatenate([xr[:half] - xr[half:], xi[:half] - xi[half:]], 0))
        sums, diffs = [], []
        for x in (even, odd):
            a, b = x[:, :half] + x[:, half:], x[:, :half] - x[:, half:]
            sums.append(jnp.concatenate([a[:half], a[half:]], 1))
            diffs.append(jnp.concatenate([b[:half], b[half:]], 1))
        fe = times(jnp.concatenate(sums, 0), *tab(0, 0))
        fo = times(jnp.concatenate(diffs, 0), *tab(1, 0))
        far[p, m, 0] = fe
        far[p, m, 1] = fo
        inten[p, :, :half] += fe[:, :half] * fe[:, :half] + fe[:, half:] * fe[:, half:]
        inten[p, :, half:] += fo[:, :half] * fo[:, :half] + fo[:, half:] * fo[:, half:]

    pair = positions

    @pl.loop(0, modes)
    def _(m):
        @pl.loop(0, positions // pair)
        def _(q):
            for i in range(pair):
                forward(q * pair + i, m)

    @pl.loop(0, positions)
    def _(p):
        moved = jnp.dot(table[8], measured[p], preferred_element_type=F32).astype(BF16)
        moved = jnp.dot(moved, table[9], preferred_element_type=F32)
        inten[p] = moved * lax.rsqrt(moved * jnp.maximum(inten[p], 0.25)) - 1.0
        pad[:, :side, :side] = jnp.zeros((2, side, side), F32)

        def inverse(m):
            se, so = inten[p, :, :half], inten[p, :, half:]
            u = times(far[p, m, 0] * jnp.concatenate([se, se], 1), *tab(0, 1))
            v = times(far[p, m, 1] * jnp.concatenate([so, so], 1), *tab(1, 1))
            a, b = u + v, u - v
            yr = jnp.concatenate([a[:, :half], b[:, :half]], 1)
            yi = jnp.concatenate([a[:, half:], b[:, half:]], 1)
            u = under(*tab(0, 0), jnp.concatenate([yr[:half], yi[:half]], 0))
            v = under(*tab(1, 0), jnp.concatenate([yr[half:], yi[half:]], 0))
            a, b = u + v, u - v
            cr = jnp.concatenate([a[:half], b[:half]], 0)
            ci = jnp.concatenate([a[half:], b[half:]], 0)
            pr, pi = probes[m, 0], probes[m, 1]
            pad[0, :side, :side] += pr * cr + pi * ci
            pad[1, :side, :side] += pr * ci - pi * cr

        for m in range(modes):
            inverse(m)

        gr, gi = pad[0, :side, :side], pad[1, :side, :side]
        wr, wi = win[p, 0, :side, :side], win[p, 1, :side, :side]
        shine = lightpad[:side, :side]
        for d in range(2):
            if d == 0:
                dr, di = win[p, 0, 1 : side + 1, :side] - wr, win[p, 1, 1 : side + 1, :side] - wi
            else:
                dr = pltpu.roll(win[p, 0, :side, :], columns - 1, 1)[:, :side] - wr
                di = pltpu.roll(win[p, 1, :side, :], columns - 1, 1)[:, :side] - wi
            nums[d, pl.ds(p, 1), :] = jnp.sum(dr * gr + di * gi, axis=0, keepdims=True)
            dens[d, pl.ds(p, 1), :] = jnp.sum((dr * dr + di * di) * shine, axis=0, keepdims=True)
        r, c = rows_ref[p], cols_ref[p]
        low = lax.rem(r, 8)
        base = pl.multiple_of(r - low, 8)
        for ch in range(2):
            x = pltpu.roll(pltpu.roll(pad[ch], c, 1), low, 0)
            frame[ch, pl.ds(base, span), :] += x

    scale = 1.0 / (side * side * modes)
    for d in range(2):
        num = jnp.sum(nums[d], axis=1, keepdims=True) * scale
        den = jnp.sum(dens[d], axis=1, keepdims=True) * scale
        steps[:, d : d + 1] = num / (den + 1e-06)


def carry_kernel(frame, grad_in, h_send, h_recv):
    tile, mode = lax.axis_index("tile"), lax.axis_index("mode")
    tiles = lax.axis_size("tile")
    side = grad_in.shape[1]
    after, before = lax.rem(tile + 1, tiles), lax.rem(tile + tiles - 1, tiles)
    barrier = pltpu.get_barrier_semaphore()
    for t in (after, before):
        pl.semaphore_signal(barrier, inc=1, **to(t, mode))
    pl.semaphore_wait(barrier, 2)
    grad_out = pltpu.make_async_remote_copy(
        src_ref=frame.at[:, frame.shape[1] - side :, :], dst_ref=grad_in,
        send_sem=h_send.at[0], recv_sem=h_recv.at[0], **to(after, mode))
    pl.when(tile < tiles - 1)(grad_out.start)
    pl.when(tile > 0)(grad_out.wait_recv)
    pl.when(tile < tiles - 1)(grad_out.wait_send)


def on_device(object_field, probe, intensities, scan_rows, scan_cols):
    tile_rows, columns = object_field.shape[1:]
    side = probe.shape[-1]
    positions = scan_rows.shape[0]
    modes = lax.axis_size("mode")
    span = side + 8
    smem = pl.BlockSpec(memory_space=pltpu.SMEM)
    vmem = pl.BlockSpec(memory_space=pltpu.VMEM)
    anywhere = pl.BlockSpec(memory_space=pl.ANY)
    dma = pltpu.SemaphoreType.DMA
    shape = jax.ShapeDtypeStruct

    following, probes, prev_rows, prev_cols = pl.pallas_call(
        gather_kernel,
        out_shape=(
            shape((2, side, columns), F32),
            shape((modes, 2, side, side), F32),
            shape((positions,), jnp.int32),
            shape((positions,), jnp.int32),
        ),
        in_specs=[anywhere] * 4,
        out_specs=(anywhere,) * 4,
        scratch_shapes=[dma((modes - 1,))] * 6 + [dma((3,))] * 2 + [dma((1,))],
        compiler_params=pltpu.CompilerParams(collective_id=0, has_side_effects=True),
    )(object_field, probe, scan_rows, scan_cols)

    frame, light, position_step = pl.pallas_call(
        compute_kernel,
        out_shape=(
            shape((2, tile_rows + side, columns), F32),
            shape((tile_rows, columns), F32),
            shape((positions, 2), F32),
        ),
        in_specs=[smem] * 4 + [anywhere] * 2 + [vmem] * 3,
        out_specs=(vmem, vmem, vmem),
        scratch_shapes=[
            pltpu.VMEM((2, tile_rows + side + 16, columns), F32),
            pltpu.VMEM((positions, 2, span, columns), F32),
            pltpu.VMEM((positions, modes, 2, side, side), F32),
            pltpu.VMEM((positions, side, side), F32),
            pltpu.VMEM((2, span, columns), F32),
            pltpu.VMEM((span, columns), F32),
            pltpu.VMEM((2 * tile_rows + side, columns), F32),
            pltpu.VMEM((2, positions, side), F32),
            pltpu.VMEM((2, positions, side), F32),
            dma((2,)),
        ],
        compiler_params=pltpu.CompilerParams(vmem_limit_bytes=52 * 1024 * 1024),
    )(
        scan_rows, scan_cols, prev_rows, prev_cols,
        object_field, following, probes, intensities, jnp.asarray(tables(side)),
    )

    carried = pl.pallas_call(
        carry_kernel,
        out_shape=shape((2, side, columns), F32),
        in_specs=[anywhere],
        out_specs=anywhere,
        scratch_shapes=[dma((1,)), dma((1,))],
        compiler_params=pltpu.CompilerParams(collective_id=1, has_side_effects=True),
    )(frame)
    carried = jnp.where(lax.axis_index("tile") > 0, carried, 0.0)

    grad = frame[:, :tile_rows] + jnp.pad(carried, ((0, 0), (0, tile_rows - side), (0, 0)))
    updated_object = object_field + grad / (light + damping)[None]
    return (updated_object, position_step)


def solution(mesh):
    in_specs = (
        P(None, "tile", None),
        P("mode", None, None, None),
        P("tile", None, None),
        P("tile"),
        P("tile"),
    )
    out_specs = (P(None, "tile", None), P("tile", None))
    return jax.shard_map(
        on_device, mesh=mesh, in_specs=in_specs, out_specs=out_specs, check_vma=False
    )
```

time: 122 us -> 76.6 us (0.63)
  waiting for transfers between devices: 47.8 us -> 0 us
  Pallas kernels: 38.2 us -> 70.4 us
  between operations: 14.2 us -> 0.75 us
  starting transfers between devices: 9.3 us -> 0 us
  local copies, waits for them, and re-layouts: 7.44 us -> 2.23 us
  other arithmetic: 4.44 us -> 2.73 us
    all_gather x1 -> x0, waiting for transfers between devices: 33.6 us -> none  [on_device(): probes = lax.all_gather(probe, 'mode', axis=0, tiled=True)]
    pallas_call x1 -> x3, Pallas kernels: 38.2 us -> 70.4 us  [the longest x1 33.3 us: on_device(): pl.pallas_call(compute_kernel, out_shape=(shape((2, tile_rows + side, col...]
    ppermute x4 -> x0, waiting for transfers between devices: 13.6 us -> none  [from_behind(): lax.ppermute(value, axis, [(source, source + steps) for source in range(f...]
    ppermute x4 -> x0, starting transfers between devices: 9.26 us -> none  [from_behind(): lax.ppermute(value, axis, [(source, source + steps) for source in range(f...]
    slice x3 -> x0, local copies, waits for them, and re-layouts: 5.15 us -> none  [the longest x1 2.66 us: on_device(): own_grad = frame[:, :tile_rows].at[:, :side].add(carried)]
    concatenate x1 -> x0, other arithmetic: 1.68 us -> none  [on_device(): jnp.concatenate([object_field, following, jnp.zeros((2, 16, columns), F32...]
    select_n x0 -> x1, other arithmetic: none -> 1.31 us  [on_device(): carried = jnp.where(lax.axis_index('tile') > 0, carried, 0.0)]
  transfers between devices with their start and end apart: 5 -> 0, of which waited for: 3 -> 0; matrix products, arithmetic and copies ran while one was open for 5% -> 0% of each run, Pallas kernels for 0% -> 0%
where the time goes in v1:
time: 76.6 us; the launch traced here: 76.1 us
  Pallas kernels  70.4 us (92%)
  other arithmetic  2.73 us (4%)
  local copies, waits for them, and re-layouts  2.23 us (3%)
    pallas_call x1, Pallas kernels, on_device(): pl.pallas_call(compute_kernel, out_shape=(shape((2, tile_rows + side, col...  33.3 us
    pallas_call x1, Pallas kernels, on_device(): pl.pallas_call(gather_kernel, out_shape=(shape((2, side, columns), F32),...  22.2 us
    pallas_call x1, Pallas kernels, on_device(): pl.pallas_call(carry_kernel, out_shape=shape((2, side, columns), F32), in...  15 us
    unnamed x15, local copies, waits for them, and re-layouts  2.23 us

profile of v1, /device:TPU:4, one launch (start us, length us, event | category | flops | bytes accessed | tf_op | source)
XLA Modules:
  0.0 76.1 jit_solution(11173385423721463686)
XLA Ops:
  0.6 0.0 copy-start.2
  0.6 0.0 copy-start.1
  0.7 0.0 copy-start
  0.7 22.2 %shard_map.77 = (f32[2,256,384]{2,1,0:T(8,128)}, f32[4,2,256,256]{3,2,1,0:T(8,128)}, s32[4]{0:T(128)}, s32[4]{0:T(128)}) custom-call(f32[2,512,384]{2,1,0:T(8,128)} %own.3, f32[1,2,256,256]{3,2,1,0:T(8,128)} %probe.1, s32[4]{0:T(128)} %rows_ref.1, s32[4]{0:T(128)} %cols_ref.1), custom_call_target="tpu_custom_call" | custom-call | tf_op jit(solution)/shard_map/pallas_call | solution.py:308
  22.8 0.0 copy-done.2
  22.9 0.0 copy-done.1
  22.9 0.0 copy-done
  22.9 0.0 copy-start.3
  22.9 0.7 copy-done.3
  23.5 0.0 copy-start.4
  23.5 0.7 copy-done.4
  24.2 33.3 %shard_map.78 = (f32[2,768,384]{2,1,0:T(8,128)}, f32[512,384]{1,0:T(8,128)S(1)}, f32[4,2]{1,0:T(4,128)S(1)}) custom-call(s32[4]{0:T(128)S(1)} %copy-done.1, s32[4]{0:T(128)S(1)} %copy-done.2, s32[4]{0:T(128)S(1)} %copy-done.3, s32[4]{0:T(128)S(1)} %copy-done.4, f32[2,512,384]{2,1,0:T(8,128)} %own.3, f32[2,256,384]{2,1,0:T(8,128)} %get-tuple-element.11.following, ...), custom_call_target="tpu_custom_call" | custom-call | tf_op jit(solution)/shard_map/pallas_call | solution.py:322
  57.5 0.0 copy-start.6
  57.5 15.0 %shard_map.79 = f32[2,256,384]{2,1,0:T(8,128)} custom-call(f32[2,768,384]{2,1,0:T(8,128)} %get-tuple-element.13.frame), custom_call_target="tpu_custom_call" | custom-call | tf_op jit(solution)/shard_map/pallas_call | solution.py:349
  72.5 0.0 copy-start.5
  72.5 1.3 %broadcast_select_fusion = f32[2,256,384]{2,1,0:T(8,128)S(1)} fusion(f32[2,256,384]{2,1,0:T(8,128)} %shard_map.79, pred[]{:T(512)S(6)} %gt.3), kind=kLoop, calls=%fused_computation.2 | loop fusion | flops 196608 | bytes 1572865 | tf_op jit(solution)/shard_map/jit(_where)/select_n | solution.py:357
  73.8 0.1 broadcast_add_fusion
  73.9 0.0 copy-done.6
  73.9 0.3 copy-done.5
  74.1 1.4 %divide_add_fusion = f32[2,512,384]{2,1,0:T(8,128)} fusion(f32[2,512,384]{2,1,0:T(8,128)S(1)} %copy-done.5, f32[2,256,384]{2,1,0:T(8,128)S(1)} %broadcast_select_fusion, f32[2,768,384]{2,1,0:T(8,128)S(1)} %copy-done.6, f32[512,384]{1,0:T(8,128)S(1)} %broadcast_add_fusion), kind=kLoop, calls=%fused_computation | loop fusion | flops 1179648 | bytes 6291456 | tf_op jit(solution)/shard_map/add | solution.py:360
  75.5 0.6 copy.8
Async XLA Ops:
  0.6 22.2 %copy-start.2 = (s32[4]{0:T(128)S(1)}, s32[4]{0:T(128)}, u32[]{:S(2)}) copy-start(s32[4]{0:T(128)} %cols_ref.1) | copy-start | bytes 52
  0.6 22.2 %copy-start.1 = (s32[4]{0:T(128)S(1)}, s32[4]{0:T(128)}, u32[]{:S(2)}) copy-start(s32[4]{0:T(128)} %rows_ref.1) | copy-start | bytes 52
  0.7 22.2 %copy-start = (bf16[4,256,256]{2,1,0:T(8,128)(2,1)S(1)}, bf16[4,256,256]{2,1,0:T(8,128)(2,1)}, u32[]{:S(2)}) copy-start(bf16[4,256,256]{2,1,0:T(8,128)(2,1)} %measured.1) | copy-start | bytes 1572868
  22.9 0.7 copy-start.3
  23.5 0.7 copy-start.4
  57.5 16.4 %copy-start.6 = (f32[2,768,384]{2,1,0:T(8,128)S(1)}, f32[2,768,384]{2,1,0:T(8,128)}, u32[]{:S(2)}) copy-start(f32[2,768,384]{2,1,0:T(8,128)} %get-tuple-element.13.frame) | copy-start | bytes 7077892
  72.5 1.6 %copy-start.5 = (f32[2,512,384]{2,1,0:T(8,128)S(1)}, f32[2,512,384]{2,1,0:T(8,128)}, u32[]{:S(2)}) copy-start(f32[2,512,384]{2,1,0:T(8,128)} %own.3) | copy-start | bytes 4718596

commit v2 on v1

--- a/solution.py
+++ b/solution.py
@@ -61,7 +61,7 @@
 
 
 def gather_kernel(
-    own, probe, scan_rows, scan_cols, following, probes, prev_rows, prev_cols,
+    own, probe, scans, following, probes, prev_scans,
     z_send, z_recv, y_send, y_recv, c_send, c_recv, h_send, h_recv, own_sem,
 ):
     tile, mode = lax.axis_index("tile"), lax.axis_index("mode")
@@ -85,12 +85,9 @@
     halo = pltpu.make_async_remote_copy(
         src_ref=own.at[:, :side, :], dst_ref=following,
         send_sem=h_send.at[0], recv_sem=h_recv.at[0], **to(before, mode))
-    send_rows = pltpu.make_async_remote_copy(
-        src_ref=scan_rows, dst_ref=prev_rows,
+    send_scans = pltpu.make_async_remote_copy(
+        src_ref=scans, dst_ref=prev_scans,
         send_sem=h_send.at[1], recv_sem=h_recv.at[1], **to(after, mode))
-    send_cols = pltpu.make_async_remote_copy(
-        src_ref=scan_cols, dst_ref=prev_cols,
-        send_sem=h_send.at[2], recv_sem=h_recv.at[2], **to(after, mode))
 
     def over_modes(k):
         return pltpu.make_async_remote_copy(
@@ -114,8 +111,7 @@
     for k in order:
         over_modes(k).start()
     pl.when(tile > 0)(halo.start)
-    send_rows.start()
-    send_cols.start()
+    send_scans.start()
     keep = pltpu.make_async_copy(probe.at[0], probes.at[mode], own_sem.at[0])
     keep.start()
     for k in order:
@@ -129,8 +125,7 @@
     keep.wait()
     pl.when(tile < tiles - 1)(halo.wait_recv)
     pl.when(tile > 0)(halo.wait_send)
-    send_rows.wait()
-    send_cols.wait()
+    send_scans.wait()
     for k in order:
         over_modes(k).wait_send()
         over_y(k).wait_send()
@@ -138,7 +133,7 @@
 
 
 def compute_kernel(
-    rows_ref, cols_ref, prev_rows_ref, prev_cols_ref, own, following, probes, measured, table,
+    rows_ref, cols_ref, prev_ref, own, following, probes, measured, table,
     frame, light, steps, ext, win, far, inten, pad, lightpad, lightbuf, nums, dens, load_sem,
 ):
     tile, tiles = lax.axis_index("tile"), lax.axis_size("tile")
@@ -180,7 +175,7 @@
     def _(p):
         add_light(rows_ref[p], cols_ref[p], tile_rows)
         first = tile == 0
-        add_light(jnp.where(first, 0, prev_rows_ref[p]), jnp.where(first, 0, prev_cols_ref[p]), 0)
+        add_light(jnp.where(first, 0, prev_ref[p]), jnp.where(first, 0, prev_ref[positions + p]), 0)
 
     load_own.wait()
     pl.when(tile < tiles - 1)(load_next.wait)
@@ -276,7 +271,7 @@
         steps[:, d : d + 1] = num / (den + 1e-06)
 
 
-def carry_kernel(frame, grad_in, h_send, h_recv):
+def carry_kernel(frame, zeros, grad_in, h_send, h_recv, zero_sem):
     tile, mode = lax.axis_index("tile"), lax.axis_index("mode")
     tiles = lax.axis_size("tile")
     side = grad_in.shape[1]
@@ -288,7 +283,10 @@
     grad_out = pltpu.make_async_remote_copy(
         src_ref=frame.at[:, frame.shape[1] - side :, :], dst_ref=grad_in,
         send_sem=h_send.at[0], recv_sem=h_recv.at[0], **to(after, mode))
+    clear = pltpu.make_async_copy(zeros, grad_in, zero_sem.at[0])
     pl.when(tile < tiles - 1)(grad_out.start)
+    pl.when(tile == 0)(clear.start)
+    pl.when(tile == 0)(clear.wait)
     pl.when(tile > 0)(grad_out.wait_recv)
     pl.when(tile < tiles - 1)(grad_out.wait_send)
 
@@ -305,19 +303,18 @@
     dma = pltpu.SemaphoreType.DMA
     shape = jax.ShapeDtypeStruct
 
-    following, probes, prev_rows, prev_cols = pl.pallas_call(
+    following, probes, prev_scans = pl.pallas_call(
         gather_kernel,
         out_shape=(
             shape((2, side, columns), F32),
             shape((modes, 2, side, side), F32),
-            shape((positions,), jnp.int32),
-            shape((positions,), jnp.int32),
+            shape((2 * positions,), jnp.int32),
         ),
-        in_specs=[anywhere] * 4,
-        out_specs=(anywhere,) * 4,
+        in_specs=[anywhere] * 3,
+        out_specs=(anywhere,) * 3,
         scratch_shapes=[dma((modes - 1,))] * 6 + [dma((3,))] * 2 + [dma((1,))],
         compiler_params=pltpu.CompilerParams(collective_id=0, has_side_effects=True),
-    )(object_field, probe, scan_rows, scan_cols)
+    )(object_field, probe, jnp.concatenate([scan_rows, scan_cols]))
 
     frame, light, position_step = pl.pallas_call(
         compute_kernel,
@@ -326,7 +323,7 @@
             shape((tile_rows, columns), F32),
             shape((positions, 2), F32),
         ),
-        in_specs=[smem] * 4 + [anywhere] * 2 + [vmem] * 3,
+        in_specs=[smem] * 3 + [anywhere] * 2 + [vmem] * 3,
         out_specs=(vmem, vmem, vmem),
         scratch_shapes=[
             pltpu.VMEM((2, tile_rows + side + 16, columns), F32),
@@ -342,19 +339,18 @@
         ],
         compiler_params=pltpu.CompilerParams(vmem_limit_bytes=52 * 1024 * 1024),
     )(
-        scan_rows, scan_cols, prev_rows, prev_cols,
+        scan_rows, scan_cols, prev_scans,
         object_field, following, probes, intensities, jnp.asarray(tables(side)),
     )
 
     carried = pl.pallas_call(
         carry_kernel,
         out_shape=shape((2, side, columns), F32),
-        in_specs=[anywhere],
+        in_specs=[anywhere] * 2,
         out_specs=anywhere,
-        scratch_shapes=[dma((1,)), dma((1,))],
+        scratch_shapes=[dma((1,))] * 3,
         compiler_params=pltpu.CompilerParams(collective_id=1, has_side_effects=True),
-    )(frame)
-    carried = jnp.where(lax.axis_index("tile") > 0, carried, 0.0)
+    )(frame, jnp.zeros((2, side, columns), F32))
 
     grad = frame[:, :tile_rows] + jnp.pad(carried, ((0, 0), (0, tile_rows - side), (0, 0)))
     updated_object = object_field + grad / (light + damping)[None]

time: 76.6 us -> 92.9 us (1.21)
  the two profiles are of different devices: /device:TPU:4 before, /device:TPU:0 now
where the time goes in v2:
time: 92.9 us; the launch traced here: 92.7 us
  Pallas kernels  84 us (90%)
  other arithmetic  4.39 us (5%)
  local copies, waits for them, and re-layouts  3.61 us (4%)
    pallas_call x1, Pallas kernels, on_device(): pl.pallas_call(compute_kernel, out_shape=(shape((2, tile_rows + side, col...  32.7 us
    pallas_call x1, Pallas kernels, on_device(): pl.pallas_call(carry_kernel, out_shape=shape((2, side, columns), F32), in...  26.5 us
    pallas_call x1, Pallas kernels, on_device(): pl.pallas_call(gather_kernel, out_shape=(shape((2, side, columns), F32),...  24.8 us
    add x2, other arithmetic, on_device(): updated_object = object_field + grad / (light + damping)[None]  3.07 us
    unnamed x11, local copies, waits for them, and re-layouts  2.67 us

profile of v2, /device:TPU:0, one launch (start us, length us, event | category | flops | bytes accessed | tf_op | source)
XLA Modules:
  0.0 92.7 jit_solution(18128578909579814974)
XLA Ops:
  0.6 0.0 copy-start.2
  0.6 0.0 copy-start.1
  0.7 0.0 copy-start
  0.7 1.3 %pad_add_fusion.scans = s32[8]{0:T(128)} fusion(s32[4]{0:T(128)} %cols_ref.1, s32[4]{0:T(128)} %rows_ref.1), kind=kLoop, calls=%fused_computation.2 | loop fusion | flops 8 | bytes 64 | tf_op jit(solution)/shard_map/concatenate | solution.py:317
  2.0 24.8 %shard_map.77 = (f32[2,256,384]{2,1,0:T(8,128)}, f32[4,2,256,256]{3,2,1,0:T(8,128)}, s32[8]{0:T(128)}) custom-call(f32[2,512,384]{2,1,0:T(8,128)} %own.3, f32[1,2,256,256]{3,2,1,0:T(8,128)} %probe.1, s32[8]{0:T(128)} %pad_add_fusion.scans), custom_call_target="tpu_custom_call" | custom-call | tf_op jit(solution)/shard_map/pallas_call | solution.py:306
  26.8 0.0 copy-done.2
  26.8 0.0 copy-done.1
  26.8 0.0 copy-done
  26.8 0.0 copy-start.3
  26.8 0.7 copy-done.3
  27.5 32.7 %shard_map.78 = (f32[2,768,384]{2,1,0:T(8,128)}, f32[512,384]{1,0:T(8,128)S(1)}, f32[4,2]{1,0:T(4,128)S(1)}) custom-call(s32[4]{0:T(128)S(1)} %copy-done.1, s32[4]{0:T(128)S(1)} %copy-done.2, s32[8]{0:T(128)S(1)} %copy-done.3, f32[2,512,384]{2,1,0:T(8,128)} %own.3, f32[2,256,384]{2,1,0:T(8,128)} %get-tuple-element.9.following, ...), custom_call_target="tpu_custom_call" | custom-call | tf_op jit(solution)/shard_map/pallas_call | solution.py:319
  60.2 0.9 %broadcast_in_dim.4.zeros = f32[2,256,384]{2,1,0:T(8,128)} broadcast(f32[]{:T(128)} %constant.3.clone.1), dimensions={} | broadcast | bytes 786436 | tf_op jit(solution)/shard_map/broadcast_in_dim | solution.py:353
  61.2 26.5 %shard_map.79 = f32[2,256,384]{2,1,0:T(8,128)} custom-call(f32[2,768,384]{2,1,0:T(8,128)} %get-tuple-element.11.frame, f32[2,256,384]{2,1,0:T(8,128)} %broadcast_in_dim.4.zeros), custom_call_target="tpu_custom_call" | custom-call | tf_op jit(solution)/shard_map/pallas_call | solution.py:346
  87.6 0.0 copy-start.4
  87.6 0.1 broadcast_add_fusion
  87.7 1.3 %copy-done.4 = f32[2,512,384]{2,1,0:T(8,128)S(1)} copy-done((f32[2,512,384]{2,1,0:T(8,128)S(1)}, f32[2,512,384]{2,1,0:T(8,128)}, u32[]{:S(2)}) %copy-start.4) | copy-done | bytes 1572888
  89.0 3.0 %divide_add_fusion = f32[2,512,384]{2,1,0:T(8,128)} fusion(f32[2,512,384]{2,1,0:T(8,128)S(1)} %copy-done.4, f32[2,256,384]{2,1,0:T(8,128)} %shard_map.79, f32[2,768,384]{2,1,0:T(8,128)} %get-tuple-element.11.frame, f32[512,384]{1,0:T(8,128)S(1)} %broadcast_add_fusion), kind=kLoop, calls=%fused_computation | loop fusion | flops 1179648 | bytes 6291456 | tf_op jit(solution)/shard_map/add | solution.py:356
  92.1 0.6 copy.8
Async XLA Ops:
  0.6 26.2 %copy-start.2 = (s32[4]{0:T(128)S(1)}, s32[4]{0:T(128)}, u32[]{:S(2)}) copy-start(s32[4]{0:T(128)} %cols_ref.1) | copy-start | bytes 52
  0.6 26.2 %copy-start.1 = (s32[4]{0:T(128)S(1)}, s32[4]{0:T(128)}, u32[]{:S(2)}) copy-start(s32[4]{0:T(128)} %rows_ref.1) | copy-start | bytes 52
  0.7 26.2 %copy-start = (bf16[4,256,256]{2,1,0:T(8,128)(2,1)S(1)}, bf16[4,256,256]{2,1,0:T(8,128)(2,1)}, u32[]{:S(2)}) copy-start(bf16[4,256,256]{2,1,0:T(8,128)(2,1)} %measured.1) | copy-start | bytes 1572868
  26.8 0.7 copy-start.3
  87.6 1.4 %copy-start.4 = (f32[2,512,384]{2,1,0:T(8,128)S(1)}, f32[2,512,384]{2,1,0:T(8,128)}, u32[]{:S(2)}) copy-start(f32[2,512,384]{2,1,0:T(8,128)} %own.3) | copy-start | bytes 4718596
